TPU v7x, 32 devices: a whole 2x2x4 slice. The times are simulated.
32 devices in a mesh: dom: 8 (over y, x, core), rep: 4 (over z).
Axes of the slice: x: 2, y: 2, z: 4, core: 2. Of those that a mesh axis runs over, the one named last changes fastest.
Arguments:
- features: float32 [2048, 256], P('dom'), may hold values from -6 to 6
- tile_values: bfloat16 [8, 64, 128, 128], P('dom', 'rep'), may hold values from 0 to 0.03125
- tile_rows: int32 [8, 64], P('dom', 'rep'), may hold values from 0 to 1
- tile_cols: int32 [8, 64], P('dom', 'rep'), may hold values from 0 to 15, as said below
- weight: float32 [256, 256], replicated, may hold values from -0.375 to 0.375
- bias: float32 [256], replicated, may hold values from -3 to 3
- cotangent: float32 [2048, 256], P('dom'), may hold values from -6 to 6
Outputs:
- activations: float32 [2048, 256], P('dom')
- grad_features: float32 [2048, 256], P('dom')
- grad_weight: float32 [256, 256], replicated
- grad_bias: float32 [256], replicated
Inputs may be any that keep to these rules, and one draw needn't show every extreme that they name: `tile_cols`: within each share of 16 consecutive tiles of a partition, every tile column 0 to 15 appears exactly once.
All inputs are finite; a program needn't handle non-finite values.
Results may differ from a plain program's by a relative error of at most 0.0003.
Values sent between devices are 32-bit elements; how exact they have to be, the bound alone decides.
A program may use at most 64 MiB of HBM per device.

v0:
```python
import jax
import jax.numpy as jnp
from jax import lax
from jax.sharding import PartitionSpec as P


def body(features, tile_values, tile_rows, tile_cols, weight, bias, cotangent):
    highest = lax.Precision.HIGHEST
    values = tile_values[0].astype(jnp.float32)
    row_ids = tile_rows[0]
    col_ids = tile_cols[0]
    tile_size = values.shape[1]
    node_rows = features.shape[0]
    feat_width = features.shape[1]
    row_blocks = node_rows // tile_size
    shard_piece = lax.all_gather(features, "dom", axis=0, tiled=True)
    block_count = shard_piece.shape[0] // tile_size
    blocks = shard_piece.reshape(block_count, tile_size, feat_width)
    offsets = col_ids[:, None]
    select = (offsets == jnp.arange(block_count, dtype=jnp.int32)[None, :]).astype(jnp.float32)
    selected = jnp.einsum("sn,nif->sif", select, blocks, precision=highest)
    products = jnp.einsum("sij,sjf->sif", values, selected, precision=highest)
    row_select = (row_ids[None, :] == jnp.arange(row_blocks, dtype=jnp.int32)[:, None]).astype(
        jnp.float32
    )
    partial_rows = jnp.einsum("bs,sif->bif", row_select, products, precision=highest).reshape(
        node_rows, feat_width
    )
    aggregated = lax.psum(partial_rows, "rep")
    before = jnp.dot(aggregated, weight, precision=highest) + bias
    gate_value = jax.nn.sigmoid(before)
    output = before * gate_value
    grad_pre = cotangent * gate_value * (1.0 + before * (1.0 - gate_value))
    messages = jnp.dot(grad_pre, weight.T, precision=highest)
    weight_term = jnp.dot(aggregated.T, grad_pre, precision=highest)
    activations, messages, weight_term, bias_term = (
        output,
        messages,
        weight_term,
        jnp.sum(grad_pre, axis=0),
    )
    grad_weight, grad_bias = lax.psum((weight_term, bias_term), "dom")
    message_blocks = messages.reshape(row_blocks, tile_size, feat_width)
    picked_messages = jnp.einsum("bs,bif->sif", row_select, message_blocks, precision=highest)
    returned = jnp.einsum("sji,sjf->sif", values, picked_messages, precision=highest)
    block_count = node_rows * lax.axis_size("dom") // tile_size
    offsets = col_ids[None, :]
    select = (offsets == jnp.arange(block_count, dtype=jnp.int32)[:, None]).astype(jnp.float32)
    source_part = lax.psum_scatter(
        jnp.einsum("ns,sif->nif", select, returned, precision=highest).reshape(
            node_rows * lax.axis_size("dom"), feat_width
        ),
        "dom",
        scatter_dimension=0,
        tiled=True,
    )
    grad_features = lax.psum(source_part, "rep")
    return (activations, grad_features, grad_weight, grad_bias)


def solution(mesh):
    return jax.shard_map(
        body,
        mesh=mesh,
        in_specs=(
            P("dom", None),
            P("dom", "rep", None, None),
            P("dom", "rep"),
            P("dom", "rep"),
            P(),
            P(),
            P("dom", None),
        ),
        out_specs=(P("dom", None), P("dom", None), P(), P()),
        check_vma=False,
    )
```

profile of v0, /device:TPU:0, one launch (start us, length us, event | category | flops | bytes accessed | tf_op | source)
XLA Modules:
  0.0 246.7 jit_solution(1948898299063535947)
XLA Ops:
  7.2 0.0 copy-start
  7.2 0.0 all-gather.2.cloned.1.call-start
  7.2 0.7 all-gather.2.cloned.1.call-update
  7.9 0.0 all-reduce.4.cloned.1.call-start
  8.0 32.6 %all-gather.2.cloned.1.call-done = f32[2048,256]{1,0:T(8,128)} async-done(((f32[256,256]{1,0:T(8,128)}), f32[2048,256]{1,0:T(8,128)}) %all-gather.2.cloned.1.call-update) | async-done | bytes 2097168 | tf_op jit(solution)/shard_map/all_gather | solution.py:16
  40.5 3.9 %fusion.8 = f32[16,128,256]{2,0,1:T(8,128)S(1)} fusion(f32[16,128,256]{2,1,0:T(8,128)} %bitcast.35, s32[16]{0:T(128)} %bitcast.40), kind=kOutput, calls=%fused_computation.8 | convolution fusion | flops 100663552 | bytes 4194368 | tf_op jit(solution)/shard_map/sn,nif->sif/dot_general | solution.py:21
  44.5 0.0 copy-done
  44.5 4.1 %fusion.6 = f32[16,256,128]{2,1,0:T(8,128)} fusion(f32[16,128,256]{2,0,1:T(8,128)S(1)} %fusion.8, bf16[1,16,128,128]{3,2,1,0:T(8,128)(2,1)S(1)} %copy-done), kind=kOutput, calls=%fused_computation.6 | convolution fusion | flops 805306368 | bytes 4718592 | tf_op jit(solution)/shard_map/sij,sjf->sif/dot_general | solution.py:22
  48.5 0.0 copy-start.3
  48.5 2.2 copy.15
  50.8 0.0 copy-start.1
  50.8 0.0 copy-start.5
  50.8 0.0 copy-start.6
  50.8 0.0 copy-done.3
  50.8 0.8 fusion.2
  51.6 0.7 copy.11
  52.4 0.0 all-reduce.4.cloned.1.call-update
  52.4 0.2 reduce-scatter.2.cloned.1.call-start
  52.6 35.2 %all-reduce.4.cloned.1.call-done = f32[256,256]{1,0:T(8,128)} async-done(((f32[256,256]{1,0:T(8,128)}), f32[256,256]{1,0:T(8,128)}) %all-reduce.4.cloned.1.call-update) | async-done | bytes 262160 | tf_op jit(solution)/shard_map/psum | solution.py:29
  87.9 0.0 copy-done.1
  87.9 0.0 copy-done.5
  87.9 0.0 copy-done.6
  87.9 2.1 fusion.25
  90.0 0.4 fusion.26
  90.4 1.1 fusion.12
  91.5 2.7 %fusion.4 = f32[16,256,128]{2,1,0:T(8,128)S(1)} fusion(f32[16,128,256]{2,0,1:T(8,128)S(1)} %fusion.12, bf16[1,16,128,128]{3,2,1,0:T(8,128)(2,1)S(1)} %copy-done), kind=kOutput, calls=%fused_computation.4 | convolution fusion | flops 805306368 | bytes 4718592 | tf_op jit(solution)/shard_map/sji,sjf->sif/dot_general | solution.py:45
  94.3 0.0 copy-start.4
  94.3 2.1 copy.18
  96.4 0.0 copy-done.4
  96.4 2.7 %fusion = f32[16,128,256]{2,0,1:T(8,128)S(1)} fusion(f32[16,256,128]{1,0,2:T(8,128)} %copy.18, s32[16]{0:T(128)S(1)} %bitcast.41), kind=kOutput, calls=%fused_computation | convolution fusion | flops 100663552 | bytes 4194368 | tf_op jit(solution)/shard_map/ns,sif->nif/dot_general | solution.py:50
  99.1 2.6 %copy.12 = f32[16,128,256]{2,1,0:T(8,128)} copy(f32[16,128,256]{2,0,1:T(8,128)S(1)} %fusion) | data formatting | bytes 4194304 | tf_op jit(solution)/shard_map/ns,sif->nif/dot_general | solution.py:50
  101.6 0.0 copy-start.2
  101.6 0.0 reduce-scatter.2.cloned.1.call-update
  101.6 0.0 all-reduce.8.cloned.1.call-start
  101.7 0.9 copy-done.2
  102.6 1.3 fusion.27
  103.9 0.0 all-reduce.8.cloned.1.call-update
  103.9 0.0 all-reduce.6.cloned.1.call-start
  103.9 38.8 %reduce-scatter.2.cloned.1.call-done = f32[256,256]{1,0:T(8,128)} async-done(((f32[2048,256]{1,0:T(8,128)}), f32[256,256]{1,0:T(8,128)}) %reduce-scatter.2.cloned.1.call-update) | async-done | bytes 262160 | tf_op jit(solution)/shard_map/reduce_scatter | solution.py:49
  142.8 0.0 all-reduce.6.cloned.1.call-update
  142.8 13.2 %psum.31 = f32[256]{0:T(256)} all-reduce(f32[256]{0:T(256)S(1)} %get-tuple-element.4), channel_id=1, replica_groups=mesh['dom'=8,'rep'=4] {'dom'}, use_global_device_ids=true, to_apply=%region_5.0 | all-reduce | flops 256 | bytes 2048 | tf_op jit(solution)/shard_map/psum | solution.py:42
  156.0 43.8 %all-reduce.8.cloned.1.call-done = f32[256,256]{1,0:T(8,128)} async-done(((f32[256,256]{1,0:T(8,128)}), f32[256,256]{1,0:T(8,128)}) %all-reduce.8.cloned.1.call-update) | async-done | bytes 262160 | tf_op jit(solution)/shard_map/psum | solution.py:42
  199.8 37.0 %all-reduce.6.cloned.1.call-done = f32[256,256]{1,0:T(8,128)} async-done(((f32[256,256]{1,0:T(8,128)}), f32[256,256]{1,0:T(8,128)}) %all-reduce.6.cloned.1.call-update) | async-done | bytes 262160 | tf_op jit(solution)/shard_map/psum | solution.py:57
  236.8 1.7 copy.30
  238.5 1.7 copy.31
Async XLA Ops:
  7.2 37.3 %copy-start = (bf16[1,16,128,128]{3,2,1,0:T(8,128)(2,1)S(1)}, bf16[1,16,128,128]{3,2,1,0:T(8,128)(2,1)}, u32[]{:S(2)}) copy-start(bf16[1,16,128,128]{3,2,1,0:T(8,128)(2,1)} %param.8) | copy-start | bytes 1572868
  7.2 33.4 %all-gather.2.cloned.1.call-start = ((), (), s32[]{:S(2)}) async-start(), calls=%async_computation.1 | async-start | bytes 2359296 | tf_op jit(solution)/shard_map/all_gather | solution.py:16
  7.9 79.9 %all-reduce.4.cloned.1.call-start = ((), (), s32[]{:S(2)}) async-start(), calls=%async_computation.2 | async-start | bytes 524288 | tf_op jit(solution)/shard_map/psum | solution.py:29
  48.5 2.3 copy-start.3
  50.8 37.1 %copy-start.1 = (f32[256,256]{1,0:T(8,128)S(1)}, f32[256,256]{1,0:T(8,128)}, u32[]{:S(2)}) copy-start(f32[256,256]{1,0:T(8,128)} %param.11) | copy-start | bytes 786436
  50.8 37.0 %copy-start.5 = (f32[256,256]{1,0:T(8,128)S(1)}, f32[256,256]{1,0:T(8,128)}, u32[]{:S(2)}) copy-start(f32[256,256]{1,0:T(8,128)} %param.13) | copy-start | bytes 786436
  50.8 37.0 %copy-start.6 = (f32[256]{0:T(256)S(1)}, f32[256]{0:T(256)}, u32[]{:S(2)}) copy-start(f32[256]{0:T(256)} %param.12) | copy-start | bytes 3076
  52.4 90.4 %reduce-scatter.2.cloned.1.call-start = ((), (), s32[]{:S(2)}) async-start(), calls=%async_computation.3 | async-start | bytes 2359296 | tf_op jit(solution)/shard_map/reduce_scatter | solution.py:49
  94.3 2.1 copy-start.4
  101.6 0.9 copy-start.2
  101.6 98.2 %all-reduce.8.cloned.1.call-start = ((), (), s32[]{:S(2)}) async-start(), calls=%async_computation.5 | async-start | bytes 524288 | tf_op jit(solution)/shard_map/psum | solution.py:42
  103.9 132.9 %all-reduce.6.cloned.1.call-start = ((), (), s32[]{:S(2)}) async-start(), calls=%async_computation.4 | async-start | bytes 524288 | tf_op jit(solution)/shard_map/psum | solution.py:57
Sparse Core Ops, SparseCore 0:
  9.9 30.5 all-gather.1
  52.5 35.2 all-reduce.3
  101.8 40.9 reduce-scatter.1
  146.2 53.5 all-reduce.7
  202.1 34.6 all-reduce.5
where the time goes:
time: 247 us
  waiting for transfers between devices  188 us (76%)
  matrix products  19.2 us (8%)
  between operations  13.9 us (6%)
  blocking collectives  13.2 us (5%)
  local copies, waits for them, and re-layouts  11.8 us (5%)
    psum x1, waiting for transfers between devices, body(): grad_weight, grad_bias = lax.psum((weight_term, bias_term), 'dom')  43.8 us
    reduce_scatter x1, waiting for transfers between devices, body(): lax.psum_scatter(jnp.einsum('ns,sif->nif', select, returned, precision=hi...  38.8 us
    psum x1, waiting for transfers between devices, body(): grad_features = lax.psum(source_part, 'rep')  37 us
    psum x1, waiting for transfers between devices, body(): aggregated = lax.psum(partial_rows, 'rep')  35.2 us
    all_gather x1, waiting for transfers between devices, body(): shard_piece = lax.all_gather(features, 'dom', axis=0, tiled=True)  32.6 us
    psum x1, blocking collectives, body(): grad_weight, grad_bias = lax.psum((weight_term, bias_term), 'dom')  13.2 us
  transfers between devices with their start and end apart: 5, of which 5 were waited for; matrix products, arithmetic and copies ran while one was open for 1% of the time, Pallas kernels for 0%

commit v1 on v0

--- a/solution.py
+++ b/solution.py
@@ -54,7 +54,11 @@
         scatter_dimension=0,
         tiled=True,
     )
-    grad_features = lax.psum(source_part, "rep")
+    grad_features = source_part
+    for hop in (1, 2):
+        grad_features = grad_features + lax.ppermute(
+            grad_features, "rep", [(dev, dev ^ hop) for dev in range(4)]
+        )
     return (activations, grad_features, grad_weight, grad_bias)
 
 

time: 247 us -> 216 us (0.87)
  waiting for transfers between devices: 188 us -> 155 us
  starting transfers between devices: 0.38 us -> 4.29 us
  local copies, waits for them, and re-layouts: 11.8 us -> 9.32 us
    psum x1 -> x0, waiting for transfers between devices: 37 us -> none  [body(): grad_features = lax.psum(source_part, 'rep')]
    ppermute x0 -> x2, waiting for transfers between devices: none -> 6.76 us  [body(): lax.ppermute(grad_features, 'rep', [(dev, dev ^ hop) for dev in range(4)])]
    psum x1, waiting for transfers between devices: 43.8 us -> 38.4 us  [body(): grad_weight, grad_bias = lax.psum((weight_term, bias_term), 'dom')]
    ppermute x0 -> x2, starting transfers between devices: none -> 3.95 us  [body(): lax.ppermute(grad_features, 'rep', [(dev, dev ^ hop) for dev in range(4)])]
    unnamed x16 -> x15, local copies, waits for them, and re-layouts: 4.25 us -> 1.71 us
  transfers between devices with their start and end apart: 5 -> 6, of which waited for: 5 -> 5; matrix products, arithmetic and copies ran while one was open for 1% -> 1% of each run, Pallas kernels for 0% -> 0%
where the time goes in v1:
time: 216 us
  waiting for transfers between devices  155 us (72%)
  matrix products  19.2 us (9%)
  between operations  13.9 us (6%)
  blocking collectives  12.6 us (6%)
  local copies, waits for them, and re-layouts  9.32 us (4%)
  starting transfers between devices  4.29 us (2%)
    reduce_scatter x1, waiting for transfers between devices, body(): lax.psum_scatter(jnp.einsum('ns,sif->nif', select, returned, precision=hi...  41.1 us
    psum x1, waiting for transfers between devices, body(): grad_weight, grad_bias = lax.psum((weight_term, bias_term), 'dom')  38.4 us
    psum x1, waiting for transfers between devices, body(): aggregated = lax.psum(partial_rows, 'rep')  35.2 us
    all_gather x1, waiting for transfers between devices, body(): shard_piece = lax.all_gather(features, 'dom', axis=0, tiled=True)  32.6 us
    psum x1, blocking collectives, body(): grad_weight, grad_bias = lax.psum((weight_term, bias_term), 'dom')  12.6 us
    ppermute x2, waiting for transfers between devices, body(): lax.ppermute(grad_features, 'rep', [(dev, dev ^ hop) for dev in range(4)])  6.76 us
  transfers between devices with their start and end apart: 6, of which 5 were waited for; matrix products, arithmetic and copies ran while one was open for 1% of the time, Pallas kernels for 0%

profile of v1, /device:TPU:0, one launch (start us, length us, event | category | flops | bytes accessed | tf_op | source)
XLA Modules:
  0.0 215.9 jit_solution(10446951870493001061)
XLA Ops:
  7.2 0.0 copy-start
  7.2 0.0 all-gather.2.cloned.1.call-start
  7.2 0.7 all-gather.2.cloned.1.call-update
  7.9 0.0 all-reduce.3.cloned.1.call-start
  8.0 32.6 %all-gather.2.cloned.1.call-done = f32[2048,256]{1,0:T(8,128)} async-done(((f32[256,256]{1,0:T(8,128)}), f32[2048,256]{1,0:T(8,128)}) %all-gather.2.cloned.1.call-update) | async-done | bytes 2097168 | tf_op jit(solution)/shard_map/all_gather | solution.py:16
  40.5 3.9 %fusion.8 = f32[16,128,256]{2,0,1:T(8,128)S(1)} fusion(f32[16,128,256]{2,1,0:T(8,128)} %bitcast.35, s32[16]{0:T(128)} %bitcast.40), kind=kOutput, calls=%fused_computation.8 | convolution fusion | flops 100663552 | bytes 4194368 | tf_op jit(solution)/shard_map/sn,nif->sif/dot_general | solution.py:21
  44.5 0.0 copy-done
  44.5 4.1 %fusion.6 = f32[16,256,128]{2,1,0:T(8,128)} fusion(f32[16,128,256]{2,0,1:T(8,128)S(1)} %fusion.8, bf16[1,16,128,128]{3,2,1,0:T(8,128)(2,1)S(1)} %copy-done), kind=kOutput, calls=%fused_computation.6 | convolution fusion | flops 805306368 | bytes 4718592 | tf_op jit(solution)/shard_map/sij,sjf->sif/dot_general | solution.py:22
  48.6 0.0 copy-start.3
  48.6 2.2 %copy.15 = f32[16,256,128]{1,0,2:T(8,128)S(1)} copy(f32[16,256,128]{2,1,0:T(8,128)} %fusion.6) | data formatting | bytes 4194304 | tf_op jit(solution)/shard_map/sij,sjf->sif/dot_general | solution.py:22
  50.8 0.0 copy-start.1
  50.8 0.0 copy-start.5
  50.8 0.0 copy-start.6
  50.8 0.0 copy-done.3
  50.9 0.8 fusion.2
  51.7 0.7 copy.11
  52.4 0.0 all-reduce.3.cloned.1.call-update
  52.4 0.2 reduce-scatter.2.cloned.1.call-start
  52.6 35.2 %all-reduce.3.cloned.1.call-done = f32[256,256]{1,0:T(8,128)} async-done(((f32[256,256]{1,0:T(8,128)}), f32[256,256]{1,0:T(8,128)}) %all-reduce.3.cloned.1.call-update) | async-done | bytes 262160 | tf_op jit(solution)/shard_map/psum | solution.py:29
  87.9 0.0 copy-done.1
  87.9 0.0 copy-done.5
  87.9 0.0 copy-done.6
  87.9 2.1 fusion.25
  90.0 0.4 fusion.26
  90.4 1.1 fusion.12
  91.6 2.7 %fusion.4 = f32[16,256,128]{2,1,0:T(8,128)S(1)} fusion(f32[16,128,256]{2,0,1:T(8,128)S(1)} %fusion.12, bf16[1,16,128,128]{3,2,1,0:T(8,128)(2,1)S(1)} %copy-done), kind=kOutput, calls=%fused_computation.4 | convolution fusion | flops 805306368 | bytes 4718592 | tf_op jit(solution)/shard_map/sji,sjf->sif/dot_general | solution.py:45
  94.3 0.0 copy-start.4
  94.3 2.1 copy.18
  96.4 0.0 copy-done.4
  96.4 2.7 %fusion = f32[16,128,256]{2,0,1:T(8,128)S(1)} fusion(f32[16,256,128]{1,0,2:T(8,128)} %copy.18, s32[16]{0:T(128)S(1)} %bitcast.41), kind=kOutput, calls=%fused_computation | convolution fusion | flops 100663552 | bytes 4194368 | tf_op jit(solution)/shard_map/ns,sif->nif/dot_general | solution.py:50
  99.1 2.6 %copy.12 = f32[16,128,256]{2,1,0:T(8,128)} copy(f32[16,128,256]{2,0,1:T(8,128)S(1)} %fusion) | data formatting | bytes 4194304 | tf_op jit(solution)/shard_map/ns,sif->nif/dot_general | solution.py:50
  101.6 0.0 copy-start.2
  101.6 0.0 reduce-scatter.2.cloned.1.call-update
  101.7 0.0 all-reduce.5.cloned.1.call-start
  101.7 41.1 %reduce-scatter.2.cloned.1.call-done = f32[256,256]{1,0:T(8,128)} async-done(((f32[2048,256]{1,0:T(8,128)}), f32[256,256]{1,0:T(8,128)}) %reduce-scatter.2.cloned.1.call-update) | async-done | bytes 262160 | tf_op jit(solution)/shard_map/reduce_scatter | solution.py:49
  142.8 1.5 collective-permute-start
  144.3 6.8 %collective-permute-done = f32[256,256]{1,0:T(8,128)S(1)} collective-permute-done((f32[256,256]{1,0:T(8,128)}, f32[256,256]{1,0:T(8,128)S(1)}, u32[]{:S(2)}, u32[]{:S(2)}) %collective-permute-start) | collective-permute-done | bytes 262176 | tf_op jit(solution)/shard_map/ppermute | solution.py:59
  151.1 1.0 add.32
  152.1 2.5 %collective-permute-start.1 = (f32[256,256]{1,0:T(8,128)S(1)}, f32[256,256]{1,0:T(8,128)S(1)}, u32[]{:S(2)}, u32[]{:S(2)}) collective-permute-start(f32[256,256]{1,0:T(8,128)S(1)} %add.32), channel_id=1, source_target_pairs={{0,2},{1,3},{2,0},{3,1},{4,6},{5,7},{6,4},{7,5},{8,10},{9,11},{10,... | collective-permute-start | bytes 786440 | tf_op jit(solution)/shard_map/ppermute | solution.py:59
  154.5 0.0 copy-done.2
  154.5 1.3 fusion.27
  155.8 0.0 all-reduce.5.cloned.1.call-update
  155.9 12.6 %psum.23 = f32[256]{0:T(256)} all-reduce(f32[256]{0:T(256)S(1)} %get-tuple-element.4), channel_id=1, replica_groups=mesh['dom'=8,'rep'=4] {'dom'}, use_global_device_ids=true, to_apply=%region_4.0 | all-reduce | flops 256 | bytes 2048 | tf_op jit(solution)/shard_map/psum | solution.py:42
  168.5 0.0 collective-permute-done.1
  168.5 0.7 add.33
  169.2 38.4 %all-reduce.5.cloned.1.call-done = f32[256,256]{1,0:T(8,128)} async-done(((f32[256,256]{1,0:T(8,128)}), f32[256,256]{1,0:T(8,128)}) %all-reduce.5.cloned.1.call-update) | async-done | bytes 262160 | tf_op jit(solution)/shard_map/psum | solution.py:42
  207.7 1.7 copy.29
Async XLA Ops:
  7.2 37.3 %copy-start = (bf16[1,16,128,128]{3,2,1,0:T(8,128)(2,1)S(1)}, bf16[1,16,128,128]{3,2,1,0:T(8,128)(2,1)}, u32[]{:S(2)}) copy-start(bf16[1,16,128,128]{3,2,1,0:T(8,128)(2,1)} %param.8) | copy-start | bytes 1572868
  7.2 33.4 %all-gather.2.cloned.1.call-start = ((), (), s32[]{:S(2)}) async-start(), calls=%async_computation.1 | async-start | bytes 2359296 | tf_op jit(solution)/shard_map/all_gather | solution.py:16
  7.9 80.0 %all-reduce.3.cloned.1.call-start = ((), (), s32[]{:S(2)}) async-start(), calls=%async_computation.2 | async-start | bytes 524288 | tf_op jit(solution)/shard_map/psum | solution.py:29
  48.6 2.3 %copy-start.3 = (s32[1,16]{1,0:T(1,128)S(1)}, s32[1,16]{1,0:T(1,128)}, u32[]{:S(2)}) copy-start(s32[1,16]{1,0:T(1,128)} %param.9) | copy-start | bytes 196
  50.8 37.1 %copy-start.1 = (f32[256,256]{1,0:T(8,128)S(1)}, f32[256,256]{1,0:T(8,128)}, u32[]{:S(2)}) copy-start(f32[256,256]{1,0:T(8,128)} %param.11) | copy-start | bytes 786436
  50.8 37.0 %copy-start.5 = (f32[256,256]{1,0:T(8,128)S(1)}, f32[256,256]{1,0:T(8,128)}, u32[]{:S(2)}) copy-start(f32[256,256]{1,0:T(8,128)} %param.13) | copy-start | bytes 786436
  50.8 37.0 %copy-start.6 = (f32[256]{0:T(256)S(1)}, f32[256]{0:T(256)}, u32[]{:S(2)}) copy-start(f32[256]{0:T(256)} %param.12) | copy-start | bytes 3076
  52.4 90.4 %reduce-scatter.2.cloned.1.call-start = ((), (), s32[]{:S(2)}) async-start(), calls=%async_computation.3 | async-start | bytes 2359296 | tf_op jit(solution)/shard_map/reduce_scatter | solution.py:49
  94.3 2.1 copy-start.4
  101.6 52.9 %copy-start.2 = (f32[256,256]{1,0:T(8,128)S(1)}, f32[256,256]{1,0:T(8,128)}, u32[]{:S(2)}) copy-start(f32[256,256]{1,0:T(8,128)} %all-reduce.3.cloned.1.call-done) | copy-start | bytes 786436
  101.7 106.0 %all-reduce.5.cloned.1.call-start = ((), (), s32[]{:S(2)}) async-start(), calls=%async_computation.4 | async-start | bytes 524288 | tf_op jit(solution)/shard_map/psum | solution.py:42
  142.8 8.2 %collective-permute-start = (f32[256,256]{1,0:T(8,128)}, f32[256,256]{1,0:T(8,128)S(1)}, u32[]{:S(2)}, u32[]{:S(2)}) collective-permute-start(f32[256,256]{1,0:T(8,128)} %reduce-scatter.2.cloned.1.call-done), channel_id=1, source_target_pairs={{0,1},{1,0},{2,3},{3,2},{4,5},{5,4},{6,7},{7,6},{8,9},{9,8},{10,11... | collective-permute-start | bytes 786440 | tf_op jit(solution)/shard_map/ppermute | solution.py:59
  152.1 16.4 %collective-permute-start.1 = (f32[256,256]{1,0:T(8,128)S(1)}, f32[256,256]{1,0:T(8,128)S(1)}, u32[]{:S(2)}, u32[]{:S(2)}) collective-permute-start(f32[256,256]{1,0:T(8,128)S(1)} %add.32), channel_id=1, source_target_pairs={{0,2},{1,3},{2,0},{3,1},{4,6},{5,7},{6,4},{7,5},{8,10},{9,11},{10,... | collective-permute-start | bytes 786440 | tf_op jit(solution)/shard_map/ppermute | solution.py:59
Sparse Core Ops, SparseCore 0:
  9.9 30.5 all-gather.1
  52.5 35.2 all-reduce.2
  101.8 40.9 reduce-scatter.1
  156.0 51.6 all-reduce.4
